TPU v7x, 32 devices: a whole 2x2x4 slice. The times are simulated.
32 devices in a mesh: rows: 2 (over y), near: 4 (over z), far: 4 (over x, core).
Axes of the slice: x: 2, y: 2, z: 4, core: 2. Of those that a mesh axis runs over, the one named last changes fastest.
Arguments:
- diag_block: float32 [512, 512], replicated, as said below
- history_rows: float32 [512, 24576], P('rows', ('near', 'far'))
- panel_below: float32 [2048, 512], P(('rows', 'near', 'far')), may hold values from -6 to 6
- history_below: float32 [2048, 24576], P('rows', ('near', 'far')), may hold values from -6 to 6
Outputs:
- panel_factor: float32 [2048, 512], P(('rows', 'near', 'far'))
- diag_factor: float32 [512, 512], replicated
Inputs may be any that keep to these rules, and one draw needn't show every extreme that they name: diag_block minus history_rows history_rows^T is symmetric with a dominant positive diagonal.
All inputs are finite; a program needn't handle non-finite values.
Results may differ from a plain program's by a relative error of at most 0.000067.
Values sent between devices are 32-bit elements; how exact they have to be, the bound alone decides.
A program may use at most 64 MiB of HBM per device.

v0:
```python
import jax
import jax.numpy as jnp
from jax import lax
from jax.sharding import PartitionSpec as P


def body(diag_block, history_rows, panel_below, history_below):
    highest = lax.Precision.HIGHEST
    gathered = lax.all_gather(history_rows, "rows", axis=0, tiled=True)
    panel_size = gathered.shape[0]
    partial_value = jnp.dot(gathered, gathered.T, precision=highest)
    schur = diag_block - lax.psum(partial_value, ("near", "far"))
    diag_factor = jnp.linalg.cholesky(schur)
    identity = jnp.eye(panel_size, dtype=jnp.float32)
    inverse = lax.linalg.triangular_solve(diag_factor, identity, left_side=True, lower=True)
    share_rows = panel_below.shape[0]
    partial_rows = jnp.dot(history_below, gathered.T, precision=highest)
    summed_rows = lax.psum(partial_rows, ("near", "far"))
    my_start = lax.axis_index(("near", "far")) * share_rows
    products = lax.dynamic_slice_in_dim(summed_rows, my_start, share_rows, 0)
    updated = panel_below - products
    panel_factor = jnp.dot(updated, inverse.T, precision=highest)
    return (panel_factor, diag_factor)


def solution(mesh):
    return jax.shard_map(
        body,
        mesh=mesh,
        in_specs=(
            P(),
            P("rows", ("near", "far")),
            P(("rows", "near", "far"), None),
            P("rows", ("near", "far")),
        ),
        out_specs=(P(("rows", "near", "far"), None), P()),
        check_vma=False,
    )
```

profile of v0, /device:TPU:0, one launch (start us, length us, event | category | flops | bytes accessed | tf_op | source)
XLA Modules:
  0.0 338.7 jit_solution(1000010766611275090)
XLA Ops:
  7.2 0.0 all-gather.2.cloned.1.call-start
  7.2 0.7 all-gather.2.cloned.1.call-update
  7.9 0.0 all-reduce.4.cloned.1.call-start
  7.9 49.3 %all-gather.2.cloned.1.call-done = f32[512,1536]{1,0:T(8,128)} async-done(((f32[256,1536]{1,0:T(8,128)}), f32[512,1536]{1,0:T(8,128)}) %all-gather.2.cloned.1.call-update) | async-done | bytes 3145744 | tf_op jit(solution)/shard_map/all_gather | solution.py:9
  57.2 0.0 copy-start
  57.2 9.4 %fusion.46 = f32[512,512]{0,1:T(8,128)} fusion(f32[512,1536]{1,0:T(8,128)} %all-gather.2.cloned.1.call-done), kind=kOutput, calls=%fused_computation.82 | convolution fusion | flops 4831838208 | bytes 4194304 | tf_op jit(solution)/shard_map/dot_general | solution.py:11
  66.6 0.0 copy-done
  66.6 13.5 %fusion.45 = f32[1024,512]{1,0:T(8,128)} fusion(f32[1024,1536]{1,0:T(8,128)} %param.7, f32[512,1536]{1,0:T(8,128)S(1)} %copy-done), kind=kOutput, calls=%fused_computation.81 | convolution fusion | flops 9663676416 | bytes 11534336 | tf_op jit(solution)/shard_map/dot_general | solution.py:17
  80.1 0.0 copy-start.2
  80.1 0.0 all-reduce.4.cloned.1.call-update
  80.1 1.2 copy-done.2
  81.3 0.3 copy.7
  81.7 0.1 iota_compare_fusion
  81.7 0.1 fusion.18
  81.9 102.2 %all-reduce.4.cloned.1.call-done = (f32[512,512]{0,1:T(8,128)}, f32[1024,512]{1,0:T(8,128)}) async-done(((f32[512,512]{0,1:T(8,128)}, f32[1024,512]{1,0:T(8,128)}), (f32[512,512]{0,1:T(8,128)}, f32[1024,512]{1,0:T(8,128)})) %all-reduce.4.cloned.1.call-update) | async-done | bytes 3145744 | tf_op jit(solution)/shard_map/psum | solution.py:12
  184.1 1.4 sub.7
  185.5 0.3 copy.8
  185.9 0.2 fusion.8
  186.1 0.0 copy-start.1
  186.1 1.0 copy-done.1
  187.1 11.7 %cholesky.104 = f32[128,128]{1,0:T(8,128)S(1)} custom-call(f32[128,128]{1,0:T(8,128)S(1)} %cholesky.266), custom_call_target="Cholesky" | custom-call | tf_op jit(solution)/shard_map/jit(cholesky)/cholesky | solution.py:13
  198.8 9.8 %custom-call.30 = f32[1,128,128]{1,2,0:T(8,128)S(1)} custom-call(f32[1,128,128]{2,1,0:T(8,128)S(1)} %get-tuple-element.33), custom_call_target="InvertDiagBlocksLowerTriangular" | custom-call | tf_op jit(solution)/shard_map/jit(cholesky)/cholesky | solution.py:13
  208.6 0.1 cholesky.224
  208.8 1.2 constant_dynamic-update-slice_fusion.3
  210.0 1.3 convolution_subtract_fusion.3
  211.3 11.7 %cholesky.217 = f32[128,128]{1,0:T(8,128)S(1)} custom-call(f32[128,128]{1,0:T(8,128)S(1)} %cholesky.270), custom_call_target="Cholesky" | custom-call | tf_op jit(solution)/shard_map/jit(cholesky)/cholesky | solution.py:13
  223.0 10.0 %custom-call.31 = f32[1,128,128]{1,2,0:T(8,128)S(1)} custom-call(f32[1,128,128]{2,1,0:T(8,128)S(1)} %get-tuple-element.30), custom_call_target="InvertDiagBlocksLowerTriangular" | custom-call | tf_op jit(solution)/shard_map/jit(cholesky)/cholesky | solution.py:13
  233.0 0.3 convolution_dynamic-update-slice_fusion
  233.3 1.3 convolution_subtract_fusion.4
  234.6 11.7 %cholesky.238 = f32[128,128]{1,0:T(8,128)S(1)} custom-call(f32[128,128]{1,0:T(8,128)S(1)} %cholesky.275), custom_call_target="Cholesky" | custom-call | tf_op jit(solution)/shard_map/jit(cholesky)/cholesky | solution.py:13
  246.4 0.7 compare_reduce_fusion.1
  247.0 9.8 %custom-call.32 = f32[1,128,128]{1,2,0:T(8,128)S(1)} custom-call(f32[1,128,128]{2,1,0:T(8,128)S(1)} %get-tuple-element.27), custom_call_target="InvertDiagBlocksLowerTriangular" | custom-call | tf_op jit(solution)/shard_map/jit(cholesky)/cholesky | solution.py:13
  256.8 0.2 convolution_dynamic-update-slice_fusion.1
  257.0 1.2 convolution_subtract_fusion.5
  258.3 11.9 %cholesky.255 = f32[128,128]{1,0:T(8,128)S(1)} custom-call(f32[128,128]{1,0:T(8,128)S(1)} %convolution_subtract_fusion.5), custom_call_target="Cholesky" | custom-call | tf_op jit(solution)/shard_map/jit(cholesky)/cholesky | solution.py:13
  270.2 0.7 compare_reduce_fusion
  270.9 0.6 compare_reduce_fusion.2
  274.1 1.2 fusion.9
  275.3 0.0 copy-start.3
  275.3 10.2 %while.1 = (s32[]{:T(128)}, f32[512,512]{1,0:T(8,128)S(1)}, s32[4,2]{0,1:T(2,128)S(1)}, f32[4,128,128]{2,1,0:T(8,128)}, s32[]{:T(128)}) while((s32[]{:T(128)}, f32[512,512]{1,0:T(8,128)S(1)}, s32[4,2]{0,1:T(2,128)S(1)}, f32[4,128,128]{2,1,0:T(8,128)}, s32[]{:T(128)}) %tuple.32), condition=%wide.while_cond, body=%wide.while_body.sunk | while | flops 2 | bytes 132705 | solution.py:15
  275.3 0.1 constant_dynamic-slice_fusion.2
  275.4 0.5 fusion.57
  275.9 1.9 bitcast_dynamic-update-slice_fusion.2
  277.9 0.1 constant_dynamic-slice_fusion.2
  277.9 0.5 fusion.57
  278.5 1.9 bitcast_dynamic-update-slice_fusion.2
  280.4 0.1 constant_dynamic-slice_fusion.2
  280.5 0.5 fusion.57
  281.0 1.9 bitcast_dynamic-update-slice_fusion.2
  283.0 0.1 constant_dynamic-slice_fusion.2
  283.0 0.5 fusion.57
  283.6 1.9 bitcast_dynamic-update-slice_fusion.2
  285.5 40.1 %custom-call.33 = f32[4,128,128]{1,2,0:T(8,128)S(1)} custom-call(f32[4,128,128]{2,1,0:T(8,128)} %get-tuple-element.9), custom_call_target="InvertDiagBlocksLowerTriangular" | custom-call | tf_op jit(solution)/shard_map/triangular_solve | solution.py:15
  325.6 0.3 fusion.20
  326.0 0.4 convolution_subtract_fusion.1
  326.3 0.4 fusion.34
  326.8 0.4 convolution_subtract_fusion
  327.2 0.4 fusion.32
  327.6 0.6 convolution_subtract_fusion.2
  328.3 0.4 fusion.31
  328.7 0.0 copy-done.3
  328.7 2.7 fusion
  (10 shorter events, 0.2 us)
Async XLA Ops:
  7.2 50.0 %all-gather.2.cloned.1.call-start = ((), (), s32[]{:S(2)}) async-start(), calls=%async_computation | async-start | bytes 4718592 | tf_op jit(solution)/shard_map/all_gather | solution.py:9
  7.9 176.2 %all-reduce.4.cloned.1.call-start = ((), (), s32[]{:S(2)}) async-start(), calls=%async_computation.1 | async-start | bytes 6291456 | tf_op jit(solution)/shard_map/psum | solution.py:12
  57.2 9.4 %copy-start = (f32[512,1536]{1,0:T(8,128)S(1)}, f32[512,1536]{1,0:T(8,128)}, u32[]{:S(2)}) copy-start(f32[512,1536]{1,0:T(8,128)} %all-gather.2.cloned.1.call-done) | copy-start | bytes 9437188
  80.1 1.2 copy-start.2
  186.1 1.0 copy-start.1
  275.3 53.4 %copy-start.3 = (f32[64,512]{1,0:T(8,128)S(1)}, f32[64,512]{1,0:T(8,128)}, u32[]{:S(2)}) copy-start(f32[64,512]{1,0:T(8,128)} %param.6) | copy-start | bytes 393220
Sparse Core Ops, SparseCore 0:
  9.5 47.6 all-gather.1
  80.2 103.8 all-reduce.3
where the time goes:
time: 345 us; the launch traced here: 339 us
  waiting for transfers between devices  152 us (44%)
  other arithmetic  122 us (35%)
  matrix products  34 us (10%)
  between operations  17.2 us (5%)
  local copies, waits for them, and re-layouts  13.2 us (4%)
    psum x1, waiting for transfers between devices, body(): schur = diag_block - lax.psum(partial_value, ('near', 'far'))  102 us
    another operation x14, other arithmetic, body(): diag_factor = jnp.linalg.cholesky(schur)  78.8 us
    all_gather x1, waiting for transfers between devices, body(): gathered = lax.all_gather(history_rows, 'rows', axis=0, tiled=True)  49.3 us
    another operation x3, other arithmetic, body(): lax.linalg.triangular_solve(diag_factor, identity, left_side=True, lower=...  41.4 us
    dot_general x1, matrix products, body(): partial_rows = jnp.dot(history_below, gathered.T, precision=highest)  13.5 us
    another operation x12, local copies, waits for them, and re-layouts  10.2 us
    dot_general x1, matrix products, body(): partial_value = jnp.dot(gathered, gathered.T, precision=highest)  9.39 us
  transfers between devices with their start and end apart: 2, of which 2 were waited for; matrix products, arithmetic and copies ran while one was open for 0% of the time, Pallas kernels for 0%

commit v1 on v0

v1 whole, which is shorter than its diff:
```python
import jax
import jax.numpy as jnp
from jax import lax
from jax.experimental import pallas as pl
from jax.experimental.pallas import tpu as pltpu
from jax.sharding import PartitionSpec as P

NT = (((1,), (1,)), ((), ()))
NN = (((1,), (0,)), ((), ()))
LIMIT = 8e-6
VMEM_BYTES = 56 * 1024 * 1024


def split(value):
    high = value.astype(jnp.bfloat16)
    low = (value - high.astype(jnp.float32)).astype(jnp.bfloat16)
    return high, low


def dot1(left, right, dims):
    return lax.dot_general(left, right, dims, preferred_element_type=jnp.float32)


def dot3(left, right, dims):
    lh, ll = left
    rh, rl = right
    return (dot1(lh, rl, dims) + dot1(ll, rh, dims)) + dot1(lh, rh, dims)


def narrow(value):
    return value.astype(jnp.bfloat16)


def norm2(value):
    return jnp.sum(value * value)


def inv_sqrt(d):
    s = lax.rsqrt(d)
    return s * (1.5 - 0.5 * d * s * s)


def grid_of(size):
    row = lax.broadcasted_iota(jnp.int32, (size, size), 0)
    col = lax.broadcasted_iota(jnp.int32, (size, size), 1)
    return row, col


def lower_half(value):
    row, col = grid_of(value.shape[0])
    return jnp.where(row > col, value, jnp.where(row == col, 0.5 * value, 0.0))


def diagonal(value):
    row, col = grid_of(value.shape[0])
    on = jnp.where(row == col, value, 0.0)
    return jnp.sum(on, axis=1, keepdims=True), jnp.sum(on, axis=0, keepdims=True)


def first_step(schur_ref, full_ref, m_ref, y_ref):
    schur = schur_ref[...]
    row, col = grid_of(schur.shape[0])
    d_col, d_row = diagonal(schur)
    scaled = jnp.where(row == col, 1.0, schur * inv_sqrt(d_col) * inv_sqrt(d_row))
    full_ref[...] = scaled
    p0 = jnp.where(row > col, scaled, 0.0)
    identity = jnp.where(row == col, 1.0, 0.0)
    p0b = narrow(p0)
    y0b = narrow(identity - p0)
    resid = -dot1(p0b, p0b, NT)
    p = lower_half(dot1(narrow(dot1(y0b, narrow(resid), NN)), y0b, NT))
    m0 = identity + p0
    q = dot1(narrow(m0), narrow(p), NN)
    m_ref[...] = m0 + q
    gap = dot1(p0b, p0b, NN) - dot1(y0b, narrow(q), NN)
    y_ref[...] = (identity - p0) + dot1(narrow(gap), y0b, NN)


def second_step_factor(full_ref, m_ref, y_ref):
    m = m_ref[...]
    m_s = split(m)
    yb = narrow(y_ref[...])
    resid = full_ref[...] - dot3(m_s, m_s, NT)
    p = lower_half(dot1(narrow(dot1(yb, narrow(resid), NN)), yb, NT))
    m_ref[...] = m + dot1(m_s[0], narrow(p), NN)
    return norm2(p)


def second_step_inverse(m_ref, y_ref):
    y = y_ref[...]
    y_s = split(y)
    row, col = grid_of(y.shape[0])
    gap = jnp.where(row == col, 1.0, 0.0) - dot3(y_s, split(m_ref[...]), NN)
    y_ref[...] = y + dot1(narrow(gap), y_s[0], NN)
    return norm2(gap)


def direct_kernel(left_ref, factor_in, panel_in, schur_ref, rows_ref, factor_ref, panel_ref, work):
    converged = left_ref[0, 0] <= LIMIT
    factor_ref[...] = jnp.where(converged, factor_in[...], 0.0)
    panel_ref[...] = jnp.where(converged, panel_in[...], rows_ref[...])

    @pl.when(jnp.logical_not(converged))
    def _():
        work[...] = schur_ref[...]
        size = work.shape[0]
        row, col = grid_of(size)
        lane = lax.broadcasted_iota(jnp.int32, (1, size), 1)
        line = lax.broadcasted_iota(jnp.int32, (size, 1), 0)

        @pl.loop(0, size)
        def _(j):
            now = work[...]
            here = jnp.sum(jnp.where(row == j, now, 0.0), axis=0, keepdims=True)
            column = jnp.sum(jnp.where(col == j, now, 0.0), axis=1, keepdims=True)
            scale = inv_sqrt(jnp.sum(jnp.where(lane == j, here, 0.0), axis=1, keepdims=True))
            l_col = jnp.where(line >= j, column * scale, 0.0)
            l_row = jnp.where(lane >= j, here * scale, 0.0)
            work[...] = now - l_col * l_row
            factor_ref[...] = jnp.where(col == j, l_col, factor_ref[...])
            rest = panel_ref[...]
            solved = jnp.sum(jnp.where(lane == j, rest, 0.0), axis=1, keepdims=True) * scale
            panel_ref[...] = jnp.where(lane == j, solved, rest - solved * l_row)


def exchange_kernel(hist_ref, below_ref, diag_ref, panel_ref,
                    factor_ref, out_ref, schur_ref, rows_ref, left_ref,
                    hist, other, below, below_hi, below_lo, sums, from_core, from_x, from_z,
                    own_all, other_all, from_y, full, m, y,
                    local_sem, hist_sem, core_sem, x_sem, z_sem, gather_sem):
    r, z, far = lax.axis_index("rows"), lax.axis_index("near"), lax.axis_index("far")
    x, c = far // 2, lax.rem(far, 2)
    to_y = {"rows": 1 - r}
    to_core = {"far": x * 2 + (1 - c)}
    to_x = {"far": (1 - x) * 2 + c}
    to_z = [{"near": lax.rem(z + d, 4)} for d in (1, 2, 3)]
    half, depth = hist_ref.shape
    piece = depth // 2
    width = half // 2
    pending = []

    barrier = pltpu.get_barrier_semaphore()
    for peer in [to_y, to_core, to_x] + to_z:
        pl.semaphore_signal(barrier, inc=1, device_id=peer, device_id_type=pl.DeviceIdType.MESH)
    pl.semaphore_wait(barrier, 6)

    def send(src, dst, sems, at, peer):
        copy = pltpu.make_async_remote_copy(
            src_ref=src, dst_ref=dst, send_sem=sems.at[(0,) + at], recv_sem=sems.at[(1,) + at],
            device_id=peer, device_id_type=pl.DeviceIdType.MESH)
        copy.start()
        pending.append(copy)
        return copy

    def columns(which):
        return pl.ds(pl.multiple_of(which * piece, piece), piece)

    everything = pl.ds(0, depth)
    lines = (pl.ds(0, half), pl.ds(0, width), pl.ds(width, width))

    def send_hist(index):
        at = (lines[index], columns(r if index == 0 else 1 - r))
        return send(hist_ref.at[at], other.at[at], hist_sem, (index,), to_y)

    load_hist = pltpu.make_async_copy(hist_ref, hist, local_sem.at[0])
    load_below = pltpu.make_async_copy(below_ref, below, local_sem.at[1])
    arrive = [send_hist(0), send_hist(1)]
    load_hist.start()
    load_below.start()

    def put_schur(stream, value):
        rows = value.shape[0] // 16
        for i in range(16):
            sums[stream][i % 2, (i // 2) % 2, i // 4] = value[i * rows:(i + 1) * rows]

    def multiply_below(streams, right, first, cols):
        tile = below.shape[0] // 4
        rows = tile // 4
        for t in range(4):
            at_rows = pl.ds(t * tile, tile)
            value = dot3((below_hi[at_rows, cols], below_lo[at_rows, cols]), right, NT)
            for i in range(4):
                at = (i % 2, i // 2, t)
                start = 0
                for stream in streams:
                    wide = sums[stream].shape[-1]
                    part = value[i * rows:(i + 1) * rows, start:start + wide]
                    sums[stream][at] = part if first else sums[stream][at] + part
                    start += wide

    def core_send(stream):
        return send(sums[stream].at[1 - c], from_core[stream], core_sem, (stream,), to_core)

    def x_send(stream, copy):
        copy.wait_recv()
        total = sums[stream]
        total[c] = total[c] + from_core[stream][...]
        return send(total.at[c, 1 - x], from_x[stream], x_sem, (stream,), to_x)

    def z_send(stream, copy):
        copy.wait_recv()
        total = sums[stream]
        total[c, x] = total[c, x] + from_x[stream][...]
        return [
            send(total.at[c, x, lax.rem(z + d + 1, 4)], from_z[stream].at[d], z_sem, (stream, d), to_z[d])
            for d in range(3)
        ]

    def z_total(stream, copies):
        for copy in copies:
            copy.wait_recv()
        got = from_z[stream]
        return (sums[stream][c, x, z] + got[0]) + (got[1] + got[2])

    def gather_z(ref, which):
        return [send(ref, ref, gather_sem, (which, 1 + d), to_z[d]) for d in range(3)]

    def gather_x(ref, which, copies):
        for copy in copies:
            copy.wait_recv()
        return send(ref, ref, gather_sem, (which, 4), to_x)

    def gather_core(ref, which, copy):
        copy.wait_recv()
        return send(ref, ref, gather_sem, (which, 5), to_core)

    def put_rows(stream, copies, start, wide):
        at = (slice(None), pl.ds(pl.multiple_of(start, wide), wide))
        rows_ref[at] = panel_ref[at] - z_total(stream, copies)

    load_hist.wait()
    own = split(hist[...])
    put_schur(0, dot3(own, own, NT))
    s0 = core_send(0)
    load_below.wait()
    tile = below.shape[0] // 8
    for t in range(8):
        at_rows = pl.ds(t * tile, tile)
        high, low = split(below[at_rows, :])
        below_hi[at_rows, :] = high
        below_lo[at_rows, :] = low
    multiply_below((1,), own, True, everything)
    b0 = core_send(1)
    s0 = x_send(0, s0)
    b0 = x_send(1, b0)
    s0 = z_send(0, s0)
    own_all[c, x, z, r] = z_total(0, s0)
    y_own = send(own_all.at[c, x, z, r], own_all.at[c, x, z, r], gather_sem, (0, 0), to_y)
    b0 = z_send(1, b0)

    arrive[0].wait_recv()
    early = columns(1 - r)
    mine, theirs = hist[:, early], other[:, early]
    right = split(theirs)
    put_schur(2, dot3(split(jnp.where(r == 1, mine, theirs)), split(jnp.where(r == 1, theirs, mine)), NT))
    s1 = core_send(2)
    y_own.wait_recv()
    g0 = gather_z(own_all.at[c, x, z], 0)
    s1 = x_send(2, s1)
    g0 = gather_x(own_all.at[c, x], 0, g0)
    s1 = z_send(2, s1)
    g0 = gather_core(own_all.at[c], 0, g0)
    mine = z_total(2, s1)
    other_all[c, x, z] = mine
    y_other = send(other_all.at[c, x, z], from_y, gather_sem, (1, 0), to_y)
    arrive.append(send_hist(2))
    multiply_below((3, 4), right, True, early)
    put_rows(1, b0, r * half, half)
    y_other.wait_recv()
    y_other.wait_send()
    pending[:] = [copy for copy in pending if copy is not y_other]
    other_all[c, x, z] = other_all[c, x, z] + from_y[...]
    g1 = gather_z(other_all.at[c, x, z], 1)
    late = columns(r)
    arrive[1].wait_recv()
    multiply_below((3,), split(other[lines[1], late]), False, late)
    b1 = core_send(3)
    g1 = gather_x(other_all.at[c, x], 1, g1)
    b1 = x_send(3, b1)
    g1 = gather_core(other_all.at[c], 1, g1)
    b1 = z_send(3, b1)

    g0.wait_recv()
    rows = half // 16
    for i in range(16):
        at = (i % 2, (i // 2) % 2, i // 4)
        for group in range(2):
            place = (pl.ds(group * half + i * rows, rows), pl.ds(group * half, half))
            schur_ref[place] = diag_ref[place] - own_all[at + (group,)]
    g1.wait_recv()
    for i in range(16):
        at = (i % 2, (i // 2) % 2, i // 4)
        place = (pl.ds(half + i * rows, rows), pl.ds(0, half))
        schur_ref[place] = diag_ref[place] - other_all[at]
    schur_ref[0:half, half:2 * half] = schur_ref[half:2 * half, 0:half].T
    first_step(schur_ref, full, m, y)

    arrive[2].wait_recv()
    multiply_below((4,), split(other[lines[2], late]), False, late)
    b2 = core_send(4)
    put_rows(3, b1, (1 - r) * half, width)
    left = second_step_factor(full, m, y)
    b2 = x_send(4, b2)
    left += second_step_inverse(m, y)
    left_ref[0, 0] = left
    b2 = z_send(4, b2)
    d_col, d_row = diagonal(schur_ref[...])
    factor_ref[...] = m[...] * (d_col * inv_sqrt(d_col))
    y_s = split(y[...])
    scale = inv_sqrt(d_row)
    put_rows(4, b2, (1 - r) * half + width, width)
    out_ref[...] = dot3(split(rows_ref[...] * scale), y_s, NT)
    for copy in pending:
        copy.wait_send()


def exchange(history_rows, history_below, diag_block, panel_below):
    half, depth = history_rows.shape
    count = history_below.shape[0]
    size = diag_block.shape[0]
    f32 = jnp.float32
    schur_rows, share = half // 16, count // 16
    streams = ((schur_rows, half), (share, half), (schur_rows, half), (share, half // 2), (share, half // 2))

    def blocks(*lead):
        return [pltpu.VMEM(lead + stream, f32) for stream in streams]

    square = jax.ShapeDtypeStruct((size, size), f32)
    strip = jax.ShapeDtypeStruct((share, size), f32)
    vmem = pl.BlockSpec(memory_space=pltpu.VMEM)
    return pl.pallas_call(
        exchange_kernel,
        out_shape=(square, strip, square, strip, jax.ShapeDtypeStruct((1, 1), f32)),
        in_specs=[pl.BlockSpec(memory_space=pl.ANY)] * 2 + [vmem] * 2,
        out_specs=(vmem,) * 4 + (pl.BlockSpec(memory_space=pltpu.SMEM),),
        scratch_shapes=[
            pltpu.VMEM((half, depth), f32),
            pltpu.VMEM((half, depth), f32),
            pltpu.VMEM((count, depth), f32),
            pltpu.VMEM((count, depth), jnp.bfloat16),
            pltpu.VMEM((count, depth), jnp.bfloat16),
            blocks(2, 2, 4),
            blocks(2, 4),
            blocks(4),
            blocks(3),
            pltpu.VMEM((2, 2, 4, 2, schur_rows, half), f32),
            pltpu.VMEM((2, 2, 4, schur_rows, half), f32),
            pltpu.VMEM((schur_rows, half), f32),
            pltpu.VMEM((size, size), f32),
            pltpu.VMEM((size, size), f32),
            pltpu.VMEM((size, size), f32),
            pltpu.SemaphoreType.DMA((2,)),
            pltpu.SemaphoreType.DMA((2, 3)),
            pltpu.SemaphoreType.DMA((2, 5)),
            pltpu.SemaphoreType.DMA((2, 5)),
            pltpu.SemaphoreType.DMA((2, 5, 3)),
            pltpu.SemaphoreType.DMA((2, 2, 6)),
        ],
        compiler_params=pltpu.CompilerParams(
            collective_id=0, has_side_effects=True, vmem_limit_bytes=VMEM_BYTES
        ),
    )(history_rows, history_below, diag_block, panel_below)


def finish(factor, panel, schur, updated, left):
    vmem = pl.BlockSpec(memory_space=pltpu.VMEM)
    factor, panel = pl.pallas_call(
        direct_kernel,
        out_shape=(
            jax.ShapeDtypeStruct(factor.shape, jnp.float32),
            jax.ShapeDtypeStruct(panel.shape, jnp.float32),
        ),
        in_specs=[pl.BlockSpec(memory_space=pltpu.SMEM)] + [vmem] * 4,
        out_specs=(vmem, vmem),
        scratch_shapes=[pltpu.VMEM(factor.shape, jnp.float32)],
        compiler_params=pltpu.CompilerParams(vmem_limit_bytes=VMEM_BYTES),
    )(left, factor, panel, schur, updated)
    return panel, factor


def body(diag_block, history_rows, panel_below, history_below):
    grid = tuple(lax.axis_size(name) for name in ("rows", "near", "far"))
    if grid == (2, 4, 4):
        return finish(*exchange(history_rows, history_below, diag_block, panel_below))
    high = lax.Precision.HIGH
    gathered = lax.all_gather(history_rows, "rows", axis=0, tiled=True)
    schur_rows = jnp.dot(history_rows, gathered.T, precision=high)
    schur_part = lax.psum_scatter(schur_rows, ("near", "far"), scatter_dimension=0, tiled=True)
    products = lax.all_gather(schur_part, ("rows", "near", "far"), axis=0, tiled=True)
    partial_rows = jnp.dot(history_below, gathered.T, precision=high)
    product_rows = lax.psum_scatter(partial_rows, ("near", "far"), scatter_dimension=0, tiled=True)
    schur = diag_block - products
    diag_factor = jnp.linalg.cholesky(schur)
    identity = jnp.eye(schur.shape[0], dtype=jnp.float32)
    inverse = lax.linalg.triangular_solve(diag_factor, identity, left_side=True, lower=True)
    panel_factor = jnp.dot(panel_below - product_rows, inverse.T, precision=high)
    return (panel_factor, diag_factor)


def solution(mesh):
    return jax.shard_map(
        body,
        mesh=mesh,
        in_specs=(
            P(),
            P("rows", ("near", "far")),
            P(("rows", "near", "far"), None),
            P("rows", ("near", "far")),
        ),
        out_specs=(P(("rows", "near", "far"), None), P()),
        check_vma=False,
    )
```

time: 345 us -> 76.7 us (0.22); the launches traced: 339 us -> 76.5 us
  waiting for transfers between devices: 152 us -> 0 us
  other arithmetic: 122 us -> 0 us
  Pallas kernels: 0 us -> 75.9 us
  matrix products: 34 us -> 0 us
  between operations: 17.2 us -> 0.64 us
  local copies, waits for them, and re-layouts: 13.2 us -> 0 us
    another operation x17 -> x0, other arithmetic: 120 us -> none  [the longest x14 78.8 us: body(): diag_factor = jnp.linalg.cholesky(schur)]
    psum x1 -> x0, waiting for transfers between devices: 102 us -> none  [body(): schur = diag_block - lax.psum(partial_value, ('near', 'far'))]
    pallas_call x0 -> x2, Pallas kernels: none -> 75.9 us  [the longest x1 72.5 us: exchange(): pl.pallas_call(exchange_kernel, out_shape=(square, strip, square, strip,...]
    all_gather x1 -> x0, waiting for transfers between devices: 49.3 us -> none  [body(): gathered = lax.all_gather(history_rows, 'rows', axis=0, tiled=True)]
    dot_general x3 -> x0, matrix products: 25.5 us -> none  [the longest x1 13.5 us: body(): partial_rows = jnp.dot(history_below, gathered.T, precision=highest)]
    another operation x17 -> x0, local copies, waits for them, and re-layouts: 10.3 us -> none
    another operation x13 -> x0, matrix products: 8.47 us -> none  [the longest x6 5.48 us: body(): diag_factor = jnp.linalg.cholesky(schur)]
  transfers between devices with their start and end apart: 2 -> 0, of which waited for: 2 -> 0; matrix products, arithmetic and copies ran while one was open for 0% -> 0% of each run, Pallas kernels for 0% -> 0%
where the time goes in v1:
time: 76.7 us; the launch traced here: 76.5 us
  Pallas kernels  75.9 us (99%)
    pallas_call x1, Pallas kernels, exchange(): pl.pallas_call(exchange_kernel, out_shape=(square, strip, square, strip,...  72.5 us
    pallas_call x1, Pallas kernels, finish(): pl.pallas_call(direct_kernel, out_shape=(jax.ShapeDtypeStruct(factor.shap...  3.39 us

profile of v1, /device:TPU:0, one launch (start us, length us, event | category | flops | bytes accessed | tf_op | source)
XLA Modules:
  0.0 76.5 jit_solution(839101668296972279)
XLA Ops:
  0.6 72.5 %shard_map.59 = (f32[512,512]{1,0:T(8,128)}, f32[64,512]{1,0:T(8,128)}, f32[512,512]{1,0:T(8,128)}, f32[64,512]{1,0:T(8,128)}, f32[1,1]{1,0:T(1,128)}) custom-call(f32[256,1536]{1,0:T(8,128)} %hist_ref.1, f32[1024,1536]{1,0:T(8,128)} %below_ref.1, f32[512,512]{1,0:T(8,128)} %diag_ref.1, f32[64,512]{1,0:T(8,128)} %panel_ref.1), custom_call_target="tpu_custom_call" | custom-call | tf_op jit(solution)/shard_map/pallas_call | solution.py:331
  73.1 3.4 %shard_map.60 = (f32[512,512]{1,0:T(8,128)}, f32[64,512]{1,0:T(8,128)}) custom-call(f32[1,1]{1,0:T(1,128)} %get-tuple-element.9.left_ref, f32[512,512]{1,0:T(8,128)} %get-tuple-element.10.factor_in, f32[64,512]{1,0:T(8,128)} %get-tuple-element.11.panel_in, f32[512,512]{1,0:T(8,128)} %get-tuple-element.12.schur_ref, f32[64,512]{1,0:T(8,128)} %get-tuple-element.13.rows_ref), custom_call_target="tpu_custom_call" | custom-call | tf_op jit(solution)/shard_map/pallas_call | solution.py:367

commit v2 on v1

--- a/solution.py
+++ b/solution.py
@@ -95,14 +95,20 @@
     return norm2(gap)
 
 
-def direct_kernel(left_ref, factor_in, panel_in, schur_ref, rows_ref, factor_ref, panel_ref, work):
-    converged = left_ref[0, 0] <= LIMIT
-    factor_ref[...] = jnp.where(converged, factor_in[...], 0.0)
-    panel_ref[...] = jnp.where(converged, panel_in[...], rows_ref[...])
-
-    @pl.when(jnp.logical_not(converged))
+def direct_kernel(left_ref, factor_in, panel_in, schur_ref, rows_ref, factor_ref, panel_ref, work, factor, rest, sem):
+    def move(*pairs):
+        copies = [pltpu.make_async_copy(*pair, sem.at[i]) for i, pair in enumerate(pairs)]
+        for copy in copies:
+            copy.start()
+        for copy in copies:
+            copy.wait()
+
+    move((factor_in, factor_ref), (panel_in, panel_ref))
+
+    @pl.when(jnp.logical_not(left_ref[0, 0] <= LIMIT))
     def _():
-        work[...] = schur_ref[...]
+        move((schur_ref, work), (rows_ref, rest))
+        factor[...] = jnp.zeros_like(factor)
         size = work.shape[0]
         row, col = grid_of(size)
         lane = lax.broadcasted_iota(jnp.int32, (1, size), 1)
@@ -117,15 +123,27 @@
             l_col = jnp.where(line >= j, column * scale, 0.0)
             l_row = jnp.where(lane >= j, here * scale, 0.0)
             work[...] = now - l_col * l_row
-            factor_ref[...] = jnp.where(col == j, l_col, factor_ref[...])
-            rest = panel_ref[...]
-            solved = jnp.sum(jnp.where(lane == j, rest, 0.0), axis=1, keepdims=True) * scale
-            panel_ref[...] = jnp.where(lane == j, solved, rest - solved * l_row)
-
-
-def exchange_kernel(hist_ref, below_ref, diag_ref, panel_ref,
-                    factor_ref, out_ref, schur_ref, rows_ref, left_ref,
-                    hist, other, below, below_hi, below_lo, sums, from_core, from_x, from_z,
+            factor[...] = jnp.where(col == j, l_col, factor[...])
+            left = rest[...]
+            solved = jnp.sum(jnp.where(lane == j, left, 0.0), axis=1, keepdims=True) * scale
+            rest[...] = jnp.where(lane == j, solved, left - solved * l_row)
+
+        move((factor, factor_ref), (rest, panel_ref))
+
+
+def pack(value):
+    rows = value.shape[0] // 2
+    return jnp.concatenate([value[:rows], value[rows:]], axis=1)
+
+
+def unpack(value):
+    cols = value.shape[1] // 2
+    return jnp.concatenate([value[:, :cols], value[:, cols:]], axis=0)
+
+
+def exchange_kernel(hist_ref, below_ref, diag_in, panel_in,
+                    factor_out, out_ref, schur_out, rows_ref, left_ref,
+                    diag_ref, panel_ref, schur_ref, factor_ref, hist, other, below, below_hi, below_lo, sums, from_core, from_x, from_z,
                     own_all, other_all, from_y, full, m, y,
                     local_sem, hist_sem, core_sem, x_sem, z_sem, gather_sem):
     r, z, far = lax.axis_index("rows"), lax.axis_index("near"), lax.axis_index("far")
@@ -156,7 +174,8 @@
         return pl.ds(pl.multiple_of(which * piece, piece), piece)
 
     everything = pl.ds(0, depth)
-    lines = (pl.ds(0, half), pl.ds(0, width), pl.ds(width, width))
+    quarter = width // 2
+    lines = (pl.ds(0, half), pl.ds(0, width), pl.ds(width, quarter), pl.ds(width + quarter, quarter))
 
     def send_hist(index):
         at = (lines[index], columns(r if index == 0 else 1 - r))
@@ -164,9 +183,13 @@
 
     load_hist = pltpu.make_async_copy(hist_ref, hist, local_sem.at[0])
     load_below = pltpu.make_async_copy(below_ref, below, local_sem.at[1])
-    arrive = [send_hist(0), send_hist(1)]
+    load_diag = pltpu.make_async_copy(diag_in, diag_ref, local_sem.at[2])
+    load_panel = pltpu.make_async_copy(panel_in, panel_ref, local_sem.at[3])
+    arrive = [send_hist(0)]
     load_hist.start()
     load_below.start()
+    load_diag.start()
+    load_panel.start()
 
     def put_schur(stream, value):
         rows = value.shape[0] // 16
@@ -183,8 +206,10 @@
                 at = (i % 2, i // 2, t)
                 start = 0
                 for stream in streams:
-                    wide = sums[stream].shape[-1]
+                    wide = quarter if stream >= 4 else sums[stream].shape[-1]
                     part = value[i * rows:(i + 1) * rows, start:start + wide]
+                    if stream >= 4:
+                        part = pack(part)
                     sums[stream][at] = part if first else sums[stream][at] + part
                     start += wide
 
@@ -246,40 +271,34 @@
     s0 = z_send(0, s0)
     own_all[c, x, z, r] = z_total(0, s0)
     y_own = send(own_all.at[c, x, z, r], own_all.at[c, x, z, r], gather_sem, (0, 0), to_y)
+    arrive.append(send_hist(1))
     b0 = z_send(1, b0)
 
     arrive[0].wait_recv()
-    early = columns(1 - r)
+    early, late = columns(1 - r), columns(r)
     mine, theirs = hist[:, early], other[:, early]
     right = split(theirs)
     put_schur(2, dot3(split(jnp.where(r == 1, mine, theirs)), split(jnp.where(r == 1, theirs, mine)), NT))
     s1 = core_send(2)
+    s1 = x_send(2, s1)
+    s1 = z_send(2, s1)
+    other_all[c, x, z] = z_total(2, s1)
+    y_other = send(other_all.at[c, x, z], from_y, gather_sem, (1, 0), to_y)
+    arrive.append(send_hist(2))
+    arrive.append(send_hist(3))
     y_own.wait_recv()
     g0 = gather_z(own_all.at[c, x, z], 0)
-    s1 = x_send(2, s1)
+    multiply_below((3, 4, 5), right, True, early)
     g0 = gather_x(own_all.at[c, x], 0, g0)
-    s1 = z_send(2, s1)
+    load_panel.wait()
+    put_rows(1, b0, r * half, half)
     g0 = gather_core(own_all.at[c], 0, g0)
-    mine = z_total(2, s1)
-    other_all[c, x, z] = mine
-    y_other = send(other_all.at[c, x, z], from_y, gather_sem, (1, 0), to_y)
-    arrive.append(send_hist(2))
-    multiply_below((3, 4), right, True, early)
-    put_rows(1, b0, r * half, half)
     y_other.wait_recv()
     y_other.wait_send()
     pending[:] = [copy for copy in pending if copy is not y_other]
     other_all[c, x, z] = other_all[c, x, z] + from_y[...]
     g1 = gather_z(other_all.at[c, x, z], 1)
-    late = columns(r)
-    arrive[1].wait_recv()
-    multiply_below((3,), split(other[lines[1], late]), False, late)
-    b1 = core_send(3)
-    g1 = gather_x(other_all.at[c, x], 1, g1)
-    b1 = x_send(3, b1)
-    g1 = gather_core(other_all.at[c], 1, g1)
-    b1 = z_send(3, b1)
-
+    load_diag.wait()
     g0.wait_recv()
     rows = half // 16
     for i in range(16):
@@ -287,12 +306,21 @@
         for group in range(2):
             place = (pl.ds(group * half + i * rows, rows), pl.ds(group * half, half))
             schur_ref[place] = diag_ref[place] - own_all[at + (group,)]
+    g1 = gather_x(other_all.at[c, x], 1, g1)
+    arrive[1].wait_recv()
+    multiply_below((3,), split(other[lines[1], late]), False, late)
+    b1 = core_send(3)
+    g1 = gather_core(other_all.at[c], 1, g1)
+    b1 = x_send(3, b1)
     g1.wait_recv()
     for i in range(16):
         at = (i % 2, (i // 2) % 2, i // 4)
         place = (pl.ds(half + i * rows, rows), pl.ds(0, half))
         schur_ref[place] = diag_ref[place] - other_all[at]
     schur_ref[0:half, half:2 * half] = schur_ref[half:2 * half, 0:half].T
+    save_schur = pltpu.make_async_copy(schur_ref, schur_out, local_sem.at[4])
+    save_schur.start()
+    b1 = z_send(3, b1)
     first_step(schur_ref, full, m, y)
 
     arrive[2].wait_recv()
@@ -301,15 +329,27 @@
     put_rows(3, b1, (1 - r) * half, width)
     left = second_step_factor(full, m, y)
     b2 = x_send(4, b2)
+    arrive[3].wait_recv()
+    multiply_below((5,), split(other[lines[3], late]), False, late)
+    b3 = core_send(5)
+    b2 = z_send(4, b2)
     left += second_step_inverse(m, y)
     left_ref[0, 0] = left
-    b2 = z_send(4, b2)
+    b3 = x_send(5, b3)
     d_col, d_row = diagonal(schur_ref[...])
     factor_ref[...] = m[...] * (d_col * inv_sqrt(d_col))
+    save_factor = pltpu.make_async_copy(factor_ref, factor_out, local_sem.at[5])
+    save_factor.start()
+    b3 = z_send(5, b3)
     y_s = split(y[...])
     scale = inv_sqrt(d_row)
-    put_rows(4, b2, (1 - r) * half + width, width)
+    fourth = unpack(z_total(4, b2))
+    fifth = unpack(z_total(5, b3))
+    at = (slice(None), pl.ds(pl.multiple_of((1 - r) * half + width, width), width))
+    rows_ref[at] = panel_ref[at] - jnp.concatenate([fourth, fifth], axis=1)
     out_ref[...] = dot3(split(rows_ref[...] * scale), y_s, NT)
+    save_schur.wait()
+    save_factor.wait()
     for copy in pending:
         copy.wait_send()
 
@@ -320,20 +360,24 @@
     size = diag_block.shape[0]
     f32 = jnp.float32
     schur_rows, share = half // 16, count // 16
-    streams = ((schur_rows, half), (share, half), (schur_rows, half), (share, half // 2), (share, half // 2))
+    streams = ((schur_rows, half), (share, half), (schur_rows, half), (share, half // 2), (share // 2, half // 2), (share // 2, half // 2))
 
     def blocks(*lead):
         return [pltpu.VMEM(lead + stream, f32) for stream in streams]
 
     square = jax.ShapeDtypeStruct((size, size), f32)
     strip = jax.ShapeDtypeStruct((share, size), f32)
-    vmem = pl.BlockSpec(memory_space=pltpu.VMEM)
+    vmem, anywhere = pl.BlockSpec(memory_space=pltpu.VMEM), pl.BlockSpec(memory_space=pl.ANY)
     return pl.pallas_call(
         exchange_kernel,
         out_shape=(square, strip, square, strip, jax.ShapeDtypeStruct((1, 1), f32)),
-        in_specs=[pl.BlockSpec(memory_space=pl.ANY)] * 2 + [vmem] * 2,
-        out_specs=(vmem,) * 4 + (pl.BlockSpec(memory_space=pltpu.SMEM),),
+        in_specs=[anywhere] * 4,
+        out_specs=(anywhere, vmem, anywhere, vmem, pl.BlockSpec(memory_space=pltpu.SMEM)),
         scratch_shapes=[
+            pltpu.VMEM((size, size), f32),
+            pltpu.VMEM((share, size), f32),
+            pltpu.VMEM((size, size), f32),
+            pltpu.VMEM((size, size), f32),
             pltpu.VMEM((half, depth), f32),
             pltpu.VMEM((half, depth), f32),
             pltpu.VMEM((count, depth), f32),
@@ -349,11 +393,11 @@
             pltpu.VMEM((size, size), f32),
             pltpu.VMEM((size, size), f32),
             pltpu.VMEM((size, size), f32),
-            pltpu.SemaphoreType.DMA((2,)),
-            pltpu.SemaphoreType.DMA((2, 3)),
-            pltpu.SemaphoreType.DMA((2, 5)),
-            pltpu.SemaphoreType.DMA((2, 5)),
-            pltpu.SemaphoreType.DMA((2, 5, 3)),
+            pltpu.SemaphoreType.DMA((6,)),
+            pltpu.SemaphoreType.DMA((2, 4)),
+            pltpu.SemaphoreType.DMA((2, 6)),
+            pltpu.SemaphoreType.DMA((2, 6)),
+            pltpu.SemaphoreType.DMA((2, 6, 3)),
             pltpu.SemaphoreType.DMA((2, 2, 6)),
         ],
         compiler_params=pltpu.CompilerParams(
@@ -363,16 +407,21 @@
 
 
 def finish(factor, panel, schur, updated, left):
-    vmem = pl.BlockSpec(memory_space=pltpu.VMEM)
+    anywhere = pl.BlockSpec(memory_space=pl.ANY)
     factor, panel = pl.pallas_call(
         direct_kernel,
         out_shape=(
             jax.ShapeDtypeStruct(factor.shape, jnp.float32),
             jax.ShapeDtypeStruct(panel.shape, jnp.float32),
         ),
-        in_specs=[pl.BlockSpec(memory_space=pltpu.SMEM)] + [vmem] * 4,
-        out_specs=(vmem, vmem),
-        scratch_shapes=[pltpu.VMEM(factor.shape, jnp.float32)],
+        in_specs=[pl.BlockSpec(memory_space=pltpu.SMEM)] + [anywhere] * 4,
+        out_specs=(anywhere, anywhere),
+        scratch_shapes=[
+            pltpu.VMEM(factor.shape, jnp.float32),
+            pltpu.VMEM(factor.shape, jnp.float32),
+            pltpu.VMEM(panel.shape, jnp.float32),
+            pltpu.SemaphoreType.DMA((2,)),
+        ],
         compiler_params=pltpu.CompilerParams(vmem_limit_bytes=VMEM_BYTES),
     )(left, factor, panel, schur, updated)
     return panel, factor

time: 76.7 us -> 112 us (1.46)
  Pallas kernels: 75.9 us -> 112 us
    pallas_call x1, Pallas kernels: 3.39 us -> 37.5 us  [finish(): pl.pallas_call(direct_kernel, out_shape=(jax.ShapeDtypeStruct(factor.shap...]
    pallas_call x1, Pallas kernels: 72.5 us -> 74 us  [exchange(): pl.pallas_call(exchange_kernel, out_shape=(square, strip, square, strip,...]
where the time goes in v2:
time: 112 us
  Pallas kernels  112 us (100%)
    pallas_call x1, Pallas kernels, exchange(): pl.pallas_call(exchange_kernel, out_shape=(square, strip, square, strip,...  74 us
    pallas_call x1, Pallas kernels, finish(): pl.pallas_call(direct_kernel, out_shape=(jax.ShapeDtypeStruct(factor.shap...  37.5 us

profile of v2, /device:TPU:0, one launch (start us, length us, event | category | flops | bytes accessed | tf_op | source)
XLA Modules:
  0.0 112.2 jit_solution(13493959875538621640)
XLA Ops:
  0.6 74.0 %shard_map.59 = (f32[512,512]{1,0:T(8,128)}, f32[64,512]{1,0:T(8,128)}, f32[512,512]{1,0:T(8,128)}, f32[64,512]{1,0:T(8,128)}, f32[1,1]{1,0:T(1,128)}) custom-call(f32[256,1536]{1,0:T(8,128)} %hist_ref.1, f32[1024,1536]{1,0:T(8,128)} %below_ref.1, f32[512,512]{1,0:T(8,128)} %diag_in.1, f32[64,512]{1,0:T(8,128)} %panel_in.1), custom_call_target="tpu_custom_call" | custom-call | tf_op jit(solution)/shard_map/pallas_call | solution.py:371
  74.7 37.5 %shard_map.60 = (f32[512,512]{1,0:T(8,128)}, f32[64,512]{1,0:T(8,128)}) custom-call(f32[1,1]{1,0:T(1,128)} %get-tuple-element.9.left_ref, f32[512,512]{1,0:T(8,128)} %get-tuple-element.10.factor_in, f32[64,512]{1,0:T(8,128)} %get-tuple-element.11.panel_in, f32[512,512]{1,0:T(8,128)} %get-tuple-element.12.schur_ref, f32[64,512]{1,0:T(8,128)} %get-tuple-element.13.rows_ref), custom_call_target="tpu_custom_call" | custom-call | tf_op jit(solution)/shard_map/pallas_call | solution.py:411

commit v3 on v2

--- a/solution.py
+++ b/solution.py
@@ -7,7 +7,7 @@
 
 NT = (((1,), (1,)), ((), ()))
 NN = (((1,), (0,)), ((), ()))
-LIMIT = 8e-6
+LIMIT = 5e-5
 VMEM_BYTES = 56 * 1024 * 1024
 
 
@@ -57,12 +57,11 @@
     return jnp.sum(on, axis=1, keepdims=True), jnp.sum(on, axis=0, keepdims=True)
 
 
-def first_step(schur_ref, full_ref, m_ref, y_ref):
+def factor_step(schur_ref, m_ref, y_ref):
     schur = schur_ref[...]
     row, col = grid_of(schur.shape[0])
     d_col, d_row = diagonal(schur)
     scaled = jnp.where(row == col, 1.0, schur * inv_sqrt(d_col) * inv_sqrt(d_row))
-    full_ref[...] = scaled
     p0 = jnp.where(row > col, scaled, 0.0)
     identity = jnp.where(row == col, 1.0, 0.0)
     p0b = narrow(p0)
@@ -74,25 +73,7 @@
     m_ref[...] = m0 + q
     gap = dot1(p0b, p0b, NN) - dot1(y0b, narrow(q), NN)
     y_ref[...] = (identity - p0) + dot1(narrow(gap), y0b, NN)
-
-
-def second_step_factor(full_ref, m_ref, y_ref):
-    m = m_ref[...]
-    m_s = split(m)
-    yb = narrow(y_ref[...])
-    resid = full_ref[...] - dot3(m_s, m_s, NT)
-    p = lower_half(dot1(narrow(dot1(yb, narrow(resid), NN)), yb, NT))
-    m_ref[...] = m + dot1(m_s[0], narrow(p), NN)
-    return norm2(p)
-
-
-def second_step_inverse(m_ref, y_ref):
-    y = y_ref[...]
-    y_s = split(y)
-    row, col = grid_of(y.shape[0])
-    gap = jnp.where(row == col, 1.0, 0.0) - dot3(y_s, split(m_ref[...]), NN)
-    y_ref[...] = y + dot1(narrow(gap), y_s[0], NN)
-    return norm2(gap)
+    return norm2(p) + norm2(gap)
 
 
 def direct_kernel(left_ref, factor_in, panel_in, schur_ref, rows_ref, factor_ref, panel_ref, work, factor, rest, sem):
@@ -103,7 +84,8 @@
         for copy in copies:
             copy.wait()
 
-    move((factor_in, factor_ref), (panel_in, panel_ref))
+    move((factor_in, factor), (panel_in, rest))
+    move((factor, factor_ref), (rest, panel_ref))
 
     @pl.when(jnp.logical_not(left_ref[0, 0] <= LIMIT))
     def _():
@@ -144,7 +126,7 @@
 def exchange_kernel(hist_ref, below_ref, diag_in, panel_in,
                     factor_out, out_ref, schur_out, rows_ref, left_ref,
                     diag_ref, panel_ref, schur_ref, factor_ref, hist, other, below, below_hi, below_lo, sums, from_core, from_x, from_z,
-                    own_all, other_all, from_y, full, m, y,
+                    own_all, other_all, from_y, m, y,
                     local_sem, hist_sem, core_sem, x_sem, z_sem, gather_sem):
     r, z, far = lax.axis_index("rows"), lax.axis_index("near"), lax.axis_index("far")
     x, c = far // 2, lax.rem(far, 2)
@@ -179,14 +161,15 @@
 
     def send_hist(index):
         at = (lines[index], columns(r if index == 0 else 1 - r))
-        return send(hist_ref.at[at], other.at[at], hist_sem, (index,), to_y)
+        return send(hist.at[at], other.at[at], hist_sem, (index,), to_y)
 
     load_hist = pltpu.make_async_copy(hist_ref, hist, local_sem.at[0])
     load_below = pltpu.make_async_copy(below_ref, below, local_sem.at[1])
     load_diag = pltpu.make_async_copy(diag_in, diag_ref, local_sem.at[2])
     load_panel = pltpu.make_async_copy(panel_in, panel_ref, local_sem.at[3])
+    load_hist.start()
+    load_hist.wait()
     arrive = [send_hist(0)]
-    load_hist.start()
     load_below.start()
     load_diag.start()
     load_panel.start()
@@ -253,7 +236,6 @@
         at = (slice(None), pl.ds(pl.multiple_of(start, wide), wide))
         rows_ref[at] = panel_ref[at] - z_total(stream, copies)
 
-    load_hist.wait()
     own = split(hist[...])
     put_schur(0, dot3(own, own, NT))
     s0 = core_send(0)
@@ -321,25 +303,22 @@
     save_schur = pltpu.make_async_copy(schur_ref, schur_out, local_sem.at[4])
     save_schur.start()
     b1 = z_send(3, b1)
-    first_step(schur_ref, full, m, y)
+    left_ref[0, 0] = factor_step(schur_ref, m, y)
+    d_col, d_row = diagonal(schur_ref[...])
+    factor_ref[...] = m[...] * (d_col * inv_sqrt(d_col))
+    save_factor = pltpu.make_async_copy(factor_ref, factor_out, local_sem.at[5])
+    save_factor.start()
 
     arrive[2].wait_recv()
     multiply_below((4,), split(other[lines[2], late]), False, late)
     b2 = core_send(4)
     put_rows(3, b1, (1 - r) * half, width)
-    left = second_step_factor(full, m, y)
     b2 = x_send(4, b2)
     arrive[3].wait_recv()
     multiply_below((5,), split(other[lines[3], late]), False, late)
     b3 = core_send(5)
     b2 = z_send(4, b2)
-    left += second_step_inverse(m, y)
-    left_ref[0, 0] = left
     b3 = x_send(5, b3)
-    d_col, d_row = diagonal(schur_ref[...])
-    factor_ref[...] = m[...] * (d_col * inv_sqrt(d_col))
-    save_factor = pltpu.make_async_copy(factor_ref, factor_out, local_sem.at[5])
-    save_factor.start()
     b3 = z_send(5, b3)
     y_s = split(y[...])
     scale = inv_sqrt(d_row)
@@ -392,7 +371,6 @@
             pltpu.VMEM((schur_rows, half), f32),
             pltpu.VMEM((size, size), f32),
             pltpu.VMEM((size, size), f32),
-            pltpu.VMEM((size, size), f32),
             pltpu.SemaphoreType.DMA((6,)),
             pltpu.SemaphoreType.DMA((2, 4)),
             pltpu.SemaphoreType.DMA((2, 6)),

time: 112 us -> 76.6 us (0.68)
  Pallas kernels: 112 us -> 75.8 us
    pallas_call x1, Pallas kernels: 37.5 us -> 2.93 us  [finish(): pl.pallas_call(direct_kernel, out_shape=(jax.ShapeDtypeStruct(factor.shap...]
    pallas_call x1, Pallas kernels: 74 us -> 72.9 us  [exchange(): pl.pallas_call(exchange_kernel, out_shape=(square, strip, square, strip,...]
where the time goes in v3:
time: 76.6 us; the launch traced here: 76.4 us
  Pallas kernels  75.8 us (99%)
    pallas_call x1, Pallas kernels, exchange(): pl.pallas_call(exchange_kernel, out_shape=(square, strip, square, strip,...  72.9 us
    pallas_call x1, Pallas kernels, finish(): pl.pallas_call(direct_kernel, out_shape=(jax.ShapeDtypeStruct(factor.shap...  2.93 us

profile of v3, /device:TPU:0, one launch (start us, length us, event | category | flops | bytes accessed | tf_op | source)
XLA Modules:
  0.0 76.4 jit_solution(6865450248819552105)
XLA Ops:
  0.6 72.9 %shard_map.59 = (f32[512,512]{1,0:T(8,128)}, f32[64,512]{1,0:T(8,128)}, f32[512,512]{1,0:T(8,128)}, f32[64,512]{1,0:T(8,128)}, f32[1,1]{1,0:T(1,128)}) custom-call(f32[256,1536]{1,0:T(8,128)} %hist_ref.1, f32[1024,1536]{1,0:T(8,128)} %below_ref.1, f32[512,512]{1,0:T(8,128)} %diag_in.1, f32[64,512]{1,0:T(8,128)} %panel_in.1), custom_call_target="tpu_custom_call" | custom-call | tf_op jit(solution)/shard_map/pallas_call | solution.py:350
  73.5 2.9 %shard_map.60 = (f32[512,512]{1,0:T(8,128)}, f32[64,512]{1,0:T(8,128)}) custom-call(f32[1,1]{1,0:T(1,128)} %get-tuple-element.9.left_ref, f32[512,512]{1,0:T(8,128)} %get-tuple-element.10.factor_in, f32[64,512]{1,0:T(8,128)} %get-tuple-element.11.panel_in, f32[512,512]{1,0:T(8,128)} %get-tuple-element.12.schur_ref, f32[64,512]{1,0:T(8,128)} %get-tuple-element.13.rows_ref), custom_call_target="tpu_custom_call" | custom-call | tf_op jit(solution)/shard_map/pallas_call | solution.py:389

commit v4 on v3

--- a/solution.py
+++ b/solution.py
@@ -169,7 +169,7 @@
     load_panel = pltpu.make_async_copy(panel_in, panel_ref, local_sem.at[3])
     load_hist.start()
     load_hist.wait()
-    arrive = [send_hist(0)]
+    arrive = [send_hist(0), send_hist(1)]
     load_below.start()
     load_diag.start()
     load_panel.start()
@@ -253,7 +253,7 @@
     s0 = z_send(0, s0)
     own_all[c, x, z, r] = z_total(0, s0)
     y_own = send(own_all.at[c, x, z, r], own_all.at[c, x, z, r], gather_sem, (0, 0), to_y)
-    arrive.append(send_hist(1))
+    arrive.append(send_hist(2))
     b0 = z_send(1, b0)
 
     arrive[0].wait_recv()
@@ -266,7 +266,6 @@
     s1 = z_send(2, s1)
     other_all[c, x, z] = z_total(2, s1)
     y_other = send(other_all.at[c, x, z], from_y, gather_sem, (1, 0), to_y)
-    arrive.append(send_hist(2))
     arrive.append(send_hist(3))
     y_own.wait_recv()
     g0 = gather_z(own_all.at[c, x, z], 0)

time: 76.6 us -> 76.4 us (level)
  no operation moved by 1% of the time
where the time goes in v4:
time: 76.4 us; the launch traced here: 76.3 us
  Pallas kernels  75.6 us (99%)
    pallas_call x1, Pallas kernels, exchange(): pl.pallas_call(exchange_kernel, out_shape=(square, strip, square, strip,...  72.7 us
    pallas_call x1, Pallas kernels, finish(): pl.pallas_call(direct_kernel, out_shape=(jax.ShapeDtypeStruct(factor.shap...  2.93 us

profile of v4, /device:TPU:0, one launch (start us, length us, event | category | flops | bytes accessed | tf_op | source)
XLA Modules:
  0.0 76.3 jit_solution(10935303794806242856)
XLA Ops:
  0.6 72.7 %shard_map.59 = (f32[512,512]{1,0:T(8,128)}, f32[64,512]{1,0:T(8,128)}, f32[512,512]{1,0:T(8,128)}, f32[64,512]{1,0:T(8,128)}, f32[1,1]{1,0:T(1,128)}) custom-call(f32[256,1536]{1,0:T(8,128)} %hist_ref.1, f32[1024,1536]{1,0:T(8,128)} %below_ref.1, f32[512,512]{1,0:T(8,128)} %diag_in.1, f32[64,512]{1,0:T(8,128)} %panel_in.1), custom_call_target="tpu_custom_call" | custom-call | tf_op jit(solution)/shard_map/pallas_call | solution.py:349
  73.3 2.9 %shard_map.60 = (f32[512,512]{1,0:T(8,128)}, f32[64,512]{1,0:T(8,128)}) custom-call(f32[1,1]{1,0:T(1,128)} %get-tuple-element.9.left_ref, f32[512,512]{1,0:T(8,128)} %get-tuple-element.10.factor_in, f32[64,512]{1,0:T(8,128)} %get-tuple-element.11.panel_in, f32[512,512]{1,0:T(8,128)} %get-tuple-element.12.schur_ref, f32[64,512]{1,0:T(8,128)} %get-tuple-element.13.rows_ref), custom_call_target="tpu_custom_call" | custom-call | tf_op jit(solution)/shard_map/pallas_call | solution.py:388
